TPU v7x, 512 devices: a whole 4x4x16 slice. The times are simulated.
512 devices in a mesh: section: 4 (over y_lo, core), seq: 128 (over z, x, y_hi).
Axes of the slice: x: 4, y: 4 (y_hi: 2, y_lo: 2; y = y_hi * 2 + y_lo), z: 16, core: 2. Of those that a mesh axis runs over, the one named last changes fastest.
Arguments:
- skip_rows: bfloat16 [4, 16384, 2048], P('section', 'seq'), may hold values from -6 to 6
- molecule_kv: bfloat16 [4, 2048, 4096], P('section', 'seq'), may hold values from -139 to 139
- norm_gain: float32 [2048], replicated, may hold values from 0.1 to 1.9
- sink_kv: float32 [2048], replicated, may hold values from -4 to 4
- w_query: bfloat16 [2048, 1024], replicated, may hold values from -0.125 to 0.125
Outputs:
- upsampled: bfloat16 [4, 16384, 1024], P('section', 'seq')
All inputs are finite; a program needn't handle non-finite values.
Results may differ from a plain program's by a relative error of at most 0.014.
The roundings to bfloat16 on the way count: a program that leaves them out, or rounds other values in their place, can miss the bound.
Values may be sent and summed in bfloat16 or wider, within the bound.
No kernel may reach another device: no remote copies, remote signals or barrier semaphores. Data moves between devices by JAX's collectives and lax.ppermute only.
A program may use at most 64 MiB of HBM per device.

v0:
```python
import jax
import jax.numpy as jnp
from jax import lax
from jax.sharding import PartitionSpec as P

NH = 16
HD = 64
SHORT = 4
BACK = 3
HQ = 1024


def passed_along(block, axis, distance):
    devices = range(lax.axis_size(axis))
    route = [((i - distance) % len(devices), i) for i in devices]
    return lax.ppermute(block, axis, route)


def from_behind(value, axis, steps):
    count = lax.axis_size(axis)
    leading, last = (max(0, -steps), min(count, count - steps))
    return lax.ppermute(value, axis, [(source, source + steps) for source in range(leading, last)])


def norm_rows(rows, gain):
    values = rows.astype(jnp.float32)
    inverse = lax.rsqrt(jnp.mean(values * values, axis=-1, keepdims=True) + 1e-06)
    return (values * inverse * gain).astype(jnp.bfloat16)


def attend(query, keyval, sink_kv, block_index, mol_dev):
    chars = query.shape[0]
    width = keyval.shape[1]
    query_heads = query.reshape(chars, NH, HD)
    keys = keyval[:HQ].reshape(NH, HD, width)
    values = keyval[HQ:].reshape(NH, HD, width)
    sink_key = sink_kv[:HQ].reshape(NH, HD)
    sink_value = sink_kv[HQ:].reshape(NH, HD)
    scores = (
        jnp.einsum("qhd,hdk->hqk", query_heads, keys, preferred_element_type=jnp.float32) * 0.125
    )
    sink = jnp.sum(query_heads.astype(jnp.float32) * sink_key[None], axis=-1).T * 0.125
    place = block_index * chars + jnp.arange(chars, dtype=jnp.int32)
    molecule = (block_index - BACK) * mol_dev + jnp.arange(width, dtype=jnp.int32)
    lag = place[:, None] - SHORT * molecule[None, :] - (SHORT - 1)
    visible = (molecule[None, :] >= 0) & (lag >= 0) & (lag < SHORT * BACK * mol_dev)
    scores = jnp.where(visible[None], scores, jnp.float32(-1e30))
    top = jnp.maximum(jnp.max(scores, axis=-1), sink)
    expo = jnp.exp(scores - top[..., None])
    sink_expo = jnp.exp(sink - top)
    total = jnp.sum(expo, axis=-1) + sink_expo
    weight = (expo / total[..., None]).astype(jnp.bfloat16)
    sink_weight = (sink_expo / total).astype(jnp.bfloat16)
    mixed = jnp.einsum("hqk,hdk->qhd", weight, values, preferred_element_type=jnp.float32)
    mixed = mixed + sink_weight.T[..., None].astype(jnp.float32) * sink_value[None]
    return mixed.reshape(chars, HQ).astype(jnp.bfloat16)


def shards(skip_rows, molecule_kv, norm_gain, sink_kv, w_query):
    arrived = passed_along(molecule_kv, "section", 1)
    normed = norm_rows(skip_rows[0], norm_gain)
    query = jnp.dot(normed, w_query, preferred_element_type=jnp.float32).astype(jnp.bfloat16)
    chars = query.shape[0]
    mol_dev = chars // SHORT
    own_block = lax.all_to_all(arrived, "seq", split_axis=2, concat_axis=1, tiled=True)[0]
    pieces = [own_block]
    current = own_block
    for step in range(BACK):
        current = from_behind(current, "seq", 1)
        pieces.insert(0, current)
    keyval = jnp.concatenate(pieces, axis=1)
    block_index = lax.axis_index("seq")
    mixed = attend(query, keyval, sink_kv, block_index, mol_dev)
    return mixed[None]


def solution(mesh):
    return jax.shard_map(
        shards,
        mesh=mesh,
        in_specs=(P("section", "seq", None), P("section", "seq", None), P(), P(), P()),
        out_specs=P("section", "seq", None),
        check_vma=False,
    )
```

profile of v0, /device:TPU:32, one launch (start us, length us, event | category | flops | bytes accessed | tf_op | source)
XLA Modules:
  0.0 130.8 jit_solution(4866062913885767191)
XLA Ops:
  0.0 2.0 %collective-permute-start = (bf16[1,16,4096]{2,1,0:T(8,128)(2,1)}, bf16[1,16,4096]{2,1,0:T(8,128)(2,1)S(1)}, u32[]{:S(2)}, u32[]{:S(2)}) collective-permute-start(bf16[1,16,4096]{2,1,0:T(8,128)(2,1)} %param.6), channel_id=1, source_target_pairs={{384,0},{0,128},{128,256},{256,384},{385,1},{1,129},{129,257},{257... | collective-permute-start | bytes 393224 | tf_op jit(solution)/shard_map/ppermute | solution.py:16
  2.1 1.2 fusion.3
  3.3 3.3 %collective-permute-done = bf16[1,16,4096]{2,1,0:T(8,128)(2,1)S(1)} collective-permute-done((bf16[1,16,4096]{2,1,0:T(8,128)(2,1)}, bf16[1,16,4096]{2,1,0:T(8,128)(2,1)S(1)}, u32[]{:S(2)}, u32[]{:S(2)}) %collective-permute-start) | collective-permute-done | bytes 131104 | tf_op jit(solution)/shard_map/ppermute | solution.py:16
  6.6 2.7 %copy.23 = bf16[1,16,4096]{1,0,2:T(2,128)(2,1)S(1)} copy(bf16[1,16,4096]{2,1,0:T(8,128)(2,1)S(1)} %collective-permute-done) | data formatting | bytes 262144 | tf_op jit(solution)/shard_map/ppermute | solution.py:16
  9.3 0.5 broadcast.85
  9.8 22.4 %reduce = bf16[4096,16]{1,0:T(8,128)(2,1)S(1)} reduce(bf16[4096,1,16]{2,1,0:T(2,128)(2,1)S(1)} %bitcast.47, bf16[]{:T(256)} %broadcast.85), dimensions={1}, to_apply=%bitcast.41.reduce_sub_computation | reduce | bytes 262146
  32.2 1.5 %reshape.119 = bf16[128,2,256]{2,1,0:T(2,128)(2,1)} reshape(bf16[4096,16]{1,0:T(8,128)(2,1)S(1)} %reduce) | data formatting | bytes 262144
  33.8 21.6 %all-to-all-start = ((bf16[128,2,256]{2,1,0:T(2,128)(2,1)}), bf16[128,2,256]{2,1,0:T(2,128)(2,1)S(1)}, u32[]{:S(2)}, u32[]{:S(2)}) async-start(bf16[128,2,256]{2,1,0:T(2,128)(2,1)} %reshape.119), calls=%async_computation | async-start | bytes 262144 | tf_op jit(solution)/shard_map/all_to_all | solution.py:65
  55.4 0.0 copy-done
  55.4 3.1 %convolution_convert_fusion = bf16[128,1024]{1,0:T(8,128)(2,1)S(1)} fusion(bf16[2048,1024]{1,0:T(8,128)(2,1)} %param.9, bf16[1,128,2048]{2,1,0:T(8,128)(2,1)} %param.5, f32[2048]{0:T(1024)S(1)} %copy-done, f32[128]{0:T(128)S(1)} %add_rsqrt_fusion), kind=kOutput, calls=%fused_computation.7 | convolution fusion | flops 538050560 | bytes 4989440 | tf_op jit(solution)/shard_map/dot_general | solution.py:62
  58.6 0.0 copy-start.1
  58.6 15.2 %all-to-all-done = bf16[128,2,256]{2,1,0:T(2,128)(2,1)S(1)} async-done(((bf16[128,2,256]{2,1,0:T(2,128)(2,1)}), bf16[128,2,256]{2,1,0:T(2,128)(2,1)S(1)}, u32[]{:S(2)}, u32[]{:S(2)}) %all-to-all-start) | async-done | bytes 131104 | tf_op jit(solution)/shard_map/all_to_all | solution.py:65
  73.8 1.8 %reshape.120 = bf16[4096,1,16]{2,1,0:T(2,128)(2,1)S(1)} reshape(bf16[128,2,256]{2,1,0:T(2,128)(2,1)S(1)} %all-to-all-done) | data formatting | bytes 262144
  75.6 2.0 %copy.24 = bf16[1,16,4096]{2,1,0:T(8,128)(2,1)S(1)} copy(bf16[1,16,4096]{1,0,2:T(2,128)(2,1)S(1)} %bitcast.48) | data formatting | bytes 262144 | tf_op jit(solution)/shard_map/all_to_all | solution.py:65
  77.6 0.4 all_to_all.12
  78.0 0.3 copy.25
  78.3 2.1 %collective-permute-start.1 = (bf16[2048,32]{1,0:T(8,128)(2,1)S(1)}, bf16[2048,32]{1,0:T(8,128)(2,1)S(1)}, u32[]{:S(2)}, u32[]{:S(2)}) collective-permute-start(bf16[2048,32]{1,0:T(8,128)(2,1)S(1)} %bitcast.50), channel_id=1, source_target_pairs={{0,1},{1,2},{2,3},{3,4},{4,5},{5,6},{6,7},{7,8},{8,9},{9,10},{10,1... | collective-permute-start | bytes 393224 | tf_op jit(solution)/shard_map/ppermute | solution.py:22
  80.5 15.4 %collective-permute-done.1 = bf16[2048,32]{1,0:T(8,128)(2,1)S(1)} collective-permute-done((bf16[2048,32]{1,0:T(8,128)(2,1)S(1)}, bf16[2048,32]{1,0:T(8,128)(2,1)S(1)}, u32[]{:S(2)}, u32[]{:S(2)}) %collective-permute-start.1) | collective-permute-done | bytes 131104 | tf_op jit(solution)/shard_map/ppermute | solution.py:22
  95.9 1.9 %collective-permute-start.2 = (bf16[2048,32]{1,0:T(8,128)(2,1)S(1)}, bf16[2048,32]{1,0:T(8,128)(2,1)S(1)}, u32[]{:S(2)}, u32[]{:S(2)}) collective-permute-start(bf16[2048,32]{1,0:T(8,128)(2,1)S(1)} %collective-permute-done.1), channel_id=1, source_target_pairs={{0,1},{1,2},{2,3},{3,4},{4,5},{5,6},{6,7},{7,8},{8,9},{9,10},{10,1... | collective-permute-start | bytes 393224 | tf_op jit(solution)/shard_map/ppermute | solution.py:22
  97.8 0.1 fusion.16
  97.9 14.6 %collective-permute-done.2 = bf16[2048,32]{1,0:T(8,128)(2,1)S(1)} collective-permute-done((bf16[2048,32]{1,0:T(8,128)(2,1)S(1)}, bf16[2048,32]{1,0:T(8,128)(2,1)S(1)}, u32[]{:S(2)}, u32[]{:S(2)}) %collective-permute-start.2) | collective-permute-done | bytes 131104 | tf_op jit(solution)/shard_map/ppermute | solution.py:22
  112.6 1.9 %collective-permute-start.3 = (bf16[2048,32]{1,0:T(8,128)(2,1)S(1)}, bf16[2048,32]{1,0:T(8,128)(2,1)S(1)}, u32[]{:S(2)}, u32[]{:S(2)}) collective-permute-start(bf16[2048,32]{1,0:T(8,128)(2,1)S(1)} %collective-permute-done.2), channel_id=1, source_target_pairs={{0,1},{1,2},{2,3},{3,4},{4,5},{5,6},{6,7},{7,8},{8,9},{9,10},{10,1... | collective-permute-start | bytes 393224 | tf_op jit(solution)/shard_map/ppermute | solution.py:22
  114.5 0.2 copy.26
  114.7 0.1 mul.88
  114.8 0.1 mul.95
  114.8 0.2 multiply_reduce_fusion
  115.0 13.2 %collective-permute-done.3 = bf16[2048,32]{1,0:T(8,128)(2,1)S(1)} collective-permute-done((bf16[2048,32]{1,0:T(8,128)(2,1)S(1)}, bf16[2048,32]{1,0:T(8,128)(2,1)S(1)}, u32[]{:S(2)}, u32[]{:S(2)}) %collective-permute-start.3) | collective-permute-done | bytes 131104 | tf_op jit(solution)/shard_map/ppermute | solution.py:22
  128.3 0.7 pad_maximum_fusion
  129.0 0.4 fusion.26
  129.4 0.2 fusion.6
  129.6 0.3 fusion.2
  129.9 0.9 copy.28
  (10 shorter events, 0.1 us)
Async XLA Ops:
  0.0 55.4 %copy-start = (f32[2048]{0:T(1024)S(1)}, f32[2048]{0:T(1024)}, u32[]{:S(2)}) copy-start(f32[2048]{0:T(1024)} %param.7) | copy-start | bytes 24580
  0.0 6.6 %collective-permute-start = (bf16[1,16,4096]{2,1,0:T(8,128)(2,1)}, bf16[1,16,4096]{2,1,0:T(8,128)(2,1)S(1)}, u32[]{:S(2)}, u32[]{:S(2)}) collective-permute-start(bf16[1,16,4096]{2,1,0:T(8,128)(2,1)} %param.6), channel_id=1, source_target_pairs={{384,0},{0,128},{128,256},{256,384},{385,1},{1,129},{129,257},{257... | collective-permute-start | bytes 393224 | tf_op jit(solution)/shard_map/ppermute | solution.py:16
  33.8 40.0 %all-to-all-start = ((bf16[128,2,256]{2,1,0:T(2,128)(2,1)}), bf16[128,2,256]{2,1,0:T(2,128)(2,1)S(1)}, u32[]{:S(2)}, u32[]{:S(2)}) async-start(bf16[128,2,256]{2,1,0:T(2,128)(2,1)} %reshape.119), calls=%async_computation | async-start | bytes 262144 | tf_op jit(solution)/shard_map/all_to_all | solution.py:65
  58.6 55.9 %copy-start.1 = (f32[2048]{0:T(1024)S(1)}, f32[2048]{0:T(1024)}, u32[]{:S(2)}) copy-start(f32[2048]{0:T(1024)} %param.8) | copy-start | bytes 24580
  78.3 17.6 %collective-permute-start.1 = (bf16[2048,32]{1,0:T(8,128)(2,1)S(1)}, bf16[2048,32]{1,0:T(8,128)(2,1)S(1)}, u32[]{:S(2)}, u32[]{:S(2)}) collective-permute-start(bf16[2048,32]{1,0:T(8,128)(2,1)S(1)} %bitcast.50), channel_id=1, source_target_pairs={{0,1},{1,2},{2,3},{3,4},{4,5},{5,6},{6,7},{7,8},{8,9},{9,10},{10,1... | collective-permute-start | bytes 393224 | tf_op jit(solution)/shard_map/ppermute | solution.py:22
  95.9 16.6 %collective-permute-start.2 = (bf16[2048,32]{1,0:T(8,128)(2,1)S(1)}, bf16[2048,32]{1,0:T(8,128)(2,1)S(1)}, u32[]{:S(2)}, u32[]{:S(2)}) collective-permute-start(bf16[2048,32]{1,0:T(8,128)(2,1)S(1)} %collective-permute-done.1), channel_id=1, source_target_pairs={{0,1},{1,2},{2,3},{3,4},{4,5},{5,6},{6,7},{7,8},{8,9},{9,10},{10,1... | collective-permute-start | bytes 393224 | tf_op jit(solution)/shard_map/ppermute | solution.py:22
  112.6 15.7 %collective-permute-start.3 = (bf16[2048,32]{1,0:T(8,128)(2,1)S(1)}, bf16[2048,32]{1,0:T(8,128)(2,1)S(1)}, u32[]{:S(2)}, u32[]{:S(2)}) collective-permute-start(bf16[2048,32]{1,0:T(8,128)(2,1)S(1)} %collective-permute-done.2), channel_id=1, source_target_pairs={{0,1},{1,2},{2,3},{3,4},{4,5},{5,6},{6,7},{7,8},{8,9},{9,10},{10,1... | collective-permute-start | bytes 393224 | tf_op jit(solution)/shard_map/ppermute | solution.py:22
where the time goes:
time: 131 us
  waiting for transfers between devices  61.9 us (47%)
  starting transfers between devices  29.6 us (23%)
  other arithmetic  24.9 us (19%)
  local copies, waits for them, and re-layouts  10.4 us (8%)
  matrix products  3.8 us (3%)
    ppermute x3, waiting for transfers between devices, from_behind(): lax.ppermute(value, axis, [(source, source + steps) for source in range(l...  43.3 us
    unnamed x1, other arithmetic  22.4 us
    all_to_all x1, starting transfers between devices, shards(): lax.all_to_all(arrived, 'seq', split_axis=2, concat_axis=1, tiled=True)[0]  21.6 us
    all_to_all x1, waiting for transfers between devices, shards(): lax.all_to_all(arrived, 'seq', split_axis=2, concat_axis=1, tiled=True)[0]  15.2 us
    ppermute x3, starting transfers between devices, from_behind(): lax.ppermute(value, axis, [(source, source + steps) for source in range(l...  5.96 us
    unnamed x7, local copies, waits for them, and re-layouts  3.87 us
    ppermute x1, waiting for transfers between devices, passed_along(): return lax.ppermute(block, axis, route)  3.33 us
    dot_general x1, matrix products, shards(): jnp.dot(normed, w_query, preferred_element_type=jnp.float32)  3.12 us
  transfers between devices with their start and end apart: 5, of which 5 were waited for; matrix products, arithmetic and copies ran while one was open for 4% of the time, Pallas kernels for 0%

commit v1 on v0

--- a/solution.py
+++ b/solution.py
@@ -62,7 +62,10 @@
     query = jnp.dot(normed, w_query, preferred_element_type=jnp.float32).astype(jnp.bfloat16)
     chars = query.shape[0]
     mol_dev = chars // SHORT
-    own_block = lax.all_to_all(arrived, "seq", split_axis=2, concat_axis=1, tiled=True)[0]
+    own_block = jnp.concatenate(
+        lax.all_to_all(jnp.stack(jnp.split(arrived, lax.axis_size("seq"), axis=2)), "seq", 0, 0),
+        axis=1,
+    )[0]
     pieces = [own_block]
     current = own_block
     for step in range(BACK):

time: 131 us -> 109 us (0.83)
  other arithmetic: 24.9 us -> 2.44 us
    unnamed x1 -> x0, other arithmetic: 22.4 us -> none
    unnamed x7 -> x131, local copies, waits for them, and re-layouts: 3.87 us -> 9.23 us
    all_to_all x3 -> x0, local copies, waits for them, and re-layouts: 2.7 us -> none  [shards(): lax.all_to_all(arrived, 'seq', split_axis=2, concat_axis=1, tiled=True)[0]]
    ppermute x1 -> x0, local copies, waits for them, and re-layouts: 2.66 us -> none  [passed_along(): return lax.ppermute(block, axis, route)]
  transfers between devices with their start and end apart: 5 -> 5, of which waited for: 5 -> 5; matrix products, arithmetic and copies ran while one was open for 4% -> 5% of each run, Pallas kernels for 0% -> 0%
where the time goes in v1:
time: 109 us; the launch traced here: 108 us
  waiting for transfers between devices  61.9 us (57%)
  starting transfers between devices  29.6 us (27%)
  local copies, waits for them, and re-layouts  10.5 us (10%)
  matrix products  3.81 us (3%)
  other arithmetic  2.44 us (2%)
    ppermute x3, waiting for transfers between devices, from_behind(): lax.ppermute(value, axis, [(source, source + steps) for source in range(l...  43.3 us
    all_to_all x1, starting transfers between devices, shards(): lax.all_to_all(jnp.stack(jnp.split(arrived, lax.axis_size('seq'), axis=2)...  21.6 us
    all_to_all x1, waiting for transfers between devices, shards(): lax.all_to_all(jnp.stack(jnp.split(arrived, lax.axis_size('seq'), axis=2)...  15.3 us
    unnamed x131, local copies, waits for them, and re-layouts  9.23 us
    ppermute x3, starting transfers between devices, from_behind(): lax.ppermute(value, axis, [(source, source + steps) for source in range(l...  5.96 us
    ppermute x1, waiting for transfers between devices, passed_along(): return lax.ppermute(block, axis, route)  3.33 us
    dot_general x1, matrix products, shards(): jnp.dot(normed, w_query, preferred_element_type=jnp.float32)  3.13 us
  transfers between devices with their start and end apart: 5, of which 5 were waited for; matrix products, arithmetic and copies ran while one was open for 5% of the time, Pallas kernels for 0%

profile of v1, /device:TPU:32, one launch (start us, length us, event | category | flops | bytes accessed | tf_op | source)
XLA Modules:
  0.0 108.5 jit_solution(9565531094496805174)
XLA Ops:
  0.0 2.0 %collective-permute-start = (bf16[1,16,4096]{2,1,0:T(8,128)(2,1)}, bf16[1,16,4096]{2,1,0:T(8,128)(2,1)S(1)}, u32[]{:S(2)}, u32[]{:S(2)}) collective-permute-start(bf16[1,16,4096]{2,1,0:T(8,128)(2,1)} %param.6), channel_id=1, source_target_pairs={{384,0},{0,128},{128,256},{256,384},{385,1},{1,129},{129,257},{257... | collective-permute-start | bytes 393224 | tf_op jit(solution)/shard_map/ppermute | solution.py:16
  2.1 1.2 %fusion.3 = f32[128]{0:T(128)S(1)} fusion(bf16[1,128,2048]{2,1,0:T(8,128)(2,1)} %param.5), kind=kLoop, calls=%fused_computation.8 | loop fusion | flops 786304 | bytes 524800 | tf_op jit(solution)/shard_map/reduce_sum | solution.py:27
  3.3 3.3 %collective-permute-done = bf16[1,16,4096]{2,1,0:T(8,128)(2,1)S(1)} collective-permute-done((bf16[1,16,4096]{2,1,0:T(8,128)(2,1)}, bf16[1,16,4096]{2,1,0:T(8,128)(2,1)S(1)}, u32[]{:S(2)}, u32[]{:S(2)}) %collective-permute-start) | collective-permute-done | bytes 131104 | tf_op jit(solution)/shard_map/ppermute | solution.py:16
  6.6 0.1 constant_dynamic-update-slice_fusion.126
  7.0 0.1 constant_dynamic-update-slice_fusion.120
  7.2 0.1 constant_dynamic-update-slice_fusion.117
  7.4 0.1 constant_dynamic-update-slice_fusion.114
  7.5 0.1 constant_dynamic-update-slice_fusion.112
  7.7 0.1 constant_dynamic-update-slice_fusion.109
  7.9 0.1 constant_dynamic-update-slice_fusion.106
  8.3 0.1 constant_dynamic-update-slice_fusion.100
  8.8 0.1 constant_dynamic-update-slice_fusion.92
  9.0 0.1 constant_dynamic-update-slice_fusion.89
  14.7 1.0 reshape.118
  15.7 21.6 %all-to-all-start = ((bf16[128,2,256]{2,1,0:T(2,128)(2,1)}), bf16[128,2,256]{2,1,0:T(2,128)(2,1)S(1)}, u32[]{:S(2)}, u32[]{:S(2)}) async-start(bf16[128,2,256]{2,1,0:T(2,128)(2,1)} %reshape.118), calls=%async_computation | async-start | bytes 262144 | tf_op jit(solution)/shard_map/all_to_all | solution.py:66
  37.4 3.1 %convolution_convert_fusion = bf16[128,1024]{1,0:T(8,128)(2,1)S(1)} fusion(bf16[2048,1024]{1,0:T(8,128)(2,1)} %param.9, bf16[1,128,2048]{2,1,0:T(8,128)(2,1)} %param.5, f32[2048]{0:T(1024)} %param.7, f32[128]{0:T(128)S(1)} %add_rsqrt_fusion), kind=kOutput, calls=%fused_computation.7 | convolution fusion | flops 538050560 | bytes 4989440 | tf_op jit(solution)/shard_map/dot_general | solution.py:62
  40.5 15.3 %all-to-all-done = bf16[128,2,256]{2,1,0:T(2,128)(2,1)S(1)} async-done(((bf16[128,2,256]{2,1,0:T(2,128)(2,1)}), bf16[128,2,256]{2,1,0:T(2,128)(2,1)S(1)}, u32[]{:S(2)}, u32[]{:S(2)}) %all-to-all-start) | async-done | bytes 131104 | tf_op jit(solution)/shard_map/all_to_all | solution.py:66
  55.8 0.3 reshape.119
  56.1 2.1 %collective-permute-start.1 = (bf16[2048,32]{1,0:T(8,128)(2,1)S(1)}, bf16[2048,32]{1,0:T(8,128)(2,1)S(1)}, u32[]{:S(2)}, u32[]{:S(2)}) collective-permute-start(bf16[2048,32]{1,0:T(8,128)(2,1)S(1)} %bitcast.557), channel_id=1, source_target_pairs={{0,1},{1,2},{2,3},{3,4},{4,5},{5,6},{6,7},{7,8},{8,9},{9,10},{10,1... | collective-permute-start | bytes 393224 | tf_op jit(solution)/shard_map/ppermute | solution.py:22
  58.2 15.4 %collective-permute-done.1 = bf16[2048,32]{1,0:T(8,128)(2,1)S(1)} collective-permute-done((bf16[2048,32]{1,0:T(8,128)(2,1)S(1)}, bf16[2048,32]{1,0:T(8,128)(2,1)S(1)}, u32[]{:S(2)}, u32[]{:S(2)}) %collective-permute-start.1) | collective-permute-done | bytes 131104 | tf_op jit(solution)/shard_map/ppermute | solution.py:22
  73.6 1.9 %collective-permute-start.2 = (bf16[2048,32]{1,0:T(8,128)(2,1)S(1)}, bf16[2048,32]{1,0:T(8,128)(2,1)S(1)}, u32[]{:S(2)}, u32[]{:S(2)}) collective-permute-start(bf16[2048,32]{1,0:T(8,128)(2,1)S(1)} %collective-permute-done.1), channel_id=1, source_target_pairs={{0,1},{1,2},{2,3},{3,4},{4,5},{5,6},{6,7},{7,8},{8,9},{9,10},{10,1... | collective-permute-start | bytes 393224 | tf_op jit(solution)/shard_map/ppermute | solution.py:22
  75.5 0.1 fusion.16
  75.7 14.6 %collective-permute-done.2 = bf16[2048,32]{1,0:T(8,128)(2,1)S(1)} collective-permute-done((bf16[2048,32]{1,0:T(8,128)(2,1)S(1)}, bf16[2048,32]{1,0:T(8,128)(2,1)S(1)}, u32[]{:S(2)}, u32[]{:S(2)}) %collective-permute-start.2) | collective-permute-done | bytes 131104 | tf_op jit(solution)/shard_map/ppermute | solution.py:22
  90.3 1.9 %collective-permute-start.3 = (bf16[2048,32]{1,0:T(8,128)(2,1)S(1)}, bf16[2048,32]{1,0:T(8,128)(2,1)S(1)}, u32[]{:S(2)}, u32[]{:S(2)}) collective-permute-start(bf16[2048,32]{1,0:T(8,128)(2,1)S(1)} %collective-permute-done.2), channel_id=1, source_target_pairs={{0,1},{1,2},{2,3},{3,4},{4,5},{5,6},{6,7},{7,8},{8,9},{9,10},{10,1... | collective-permute-start | bytes 393224 | tf_op jit(solution)/shard_map/ppermute | solution.py:22
  92.2 0.2 copy.406
  92.5 0.2 multiply_reduce_fusion
  92.8 13.2 %collective-permute-done.3 = bf16[2048,32]{1,0:T(8,128)(2,1)S(1)} collective-permute-done((bf16[2048,32]{1,0:T(8,128)(2,1)S(1)}, bf16[2048,32]{1,0:T(8,128)(2,1)S(1)}, u32[]{:S(2)}, u32[]{:S(2)}) %collective-permute-start.3) | collective-permute-done | bytes 131104 | tf_op jit(solution)/shard_map/ppermute | solution.py:22
  106.0 0.7 pad_maximum_fusion
  106.7 0.4 fusion.26
  107.1 0.2 fusion.6
  107.3 0.3 fusion.2
  107.6 0.9 copy.408
  (130 shorter events, 7.4 us)
Async XLA Ops:
  0.0 92.2 %copy-start = (f32[2048]{0:T(1024)S(1)}, f32[2048]{0:T(1024)}, u32[]{:S(2)}) copy-start(f32[2048]{0:T(1024)} %param.8) | copy-start | bytes 24580
  0.0 6.6 %collective-permute-start = (bf16[1,16,4096]{2,1,0:T(8,128)(2,1)}, bf16[1,16,4096]{2,1,0:T(8,128)(2,1)S(1)}, u32[]{:S(2)}, u32[]{:S(2)}) collective-permute-start(bf16[1,16,4096]{2,1,0:T(8,128)(2,1)} %param.6), channel_id=1, source_target_pairs={{384,0},{0,128},{128,256},{256,384},{385,1},{1,129},{129,257},{257... | collective-permute-start | bytes 393224 | tf_op jit(solution)/shard_map/ppermute | solution.py:16
  15.7 40.0 %all-to-all-start = ((bf16[128,2,256]{2,1,0:T(2,128)(2,1)}), bf16[128,2,256]{2,1,0:T(2,128)(2,1)S(1)}, u32[]{:S(2)}, u32[]{:S(2)}) async-start(bf16[128,2,256]{2,1,0:T(2,128)(2,1)} %reshape.118), calls=%async_computation | async-start | bytes 262144 | tf_op jit(solution)/shard_map/all_to_all | solution.py:66
  56.1 17.6 %collective-permute-start.1 = (bf16[2048,32]{1,0:T(8,128)(2,1)S(1)}, bf16[2048,32]{1,0:T(8,128)(2,1)S(1)}, u32[]{:S(2)}, u32[]{:S(2)}) collective-permute-start(bf16[2048,32]{1,0:T(8,128)(2,1)S(1)} %bitcast.557), channel_id=1, source_target_pairs={{0,1},{1,2},{2,3},{3,4},{4,5},{5,6},{6,7},{7,8},{8,9},{9,10},{10,1... | collective-permute-start | bytes 393224 | tf_op jit(solution)/shard_map/ppermute | solution.py:22
  73.6 16.6 %collective-permute-start.2 = (bf16[2048,32]{1,0:T(8,128)(2,1)S(1)}, bf16[2048,32]{1,0:T(8,128)(2,1)S(1)}, u32[]{:S(2)}, u32[]{:S(2)}) collective-permute-start(bf16[2048,32]{1,0:T(8,128)(2,1)S(1)} %collective-permute-done.1), channel_id=1, source_target_pairs={{0,1},{1,2},{2,3},{3,4},{4,5},{5,6},{6,7},{7,8},{8,9},{9,10},{10,1... | collective-permute-start | bytes 393224 | tf_op jit(solution)/shard_map/ppermute | solution.py:22
  90.3 15.7 %collective-permute-start.3 = (bf16[2048,32]{1,0:T(8,128)(2,1)S(1)}, bf16[2048,32]{1,0:T(8,128)(2,1)S(1)}, u32[]{:S(2)}, u32[]{:S(2)}) collective-permute-start(bf16[2048,32]{1,0:T(8,128)(2,1)S(1)} %collective-permute-done.2), channel_id=1, source_target_pairs={{0,1},{1,2},{2,3},{3,4},{4,5},{5,6},{6,7},{7,8},{8,9},{9,10},{10,1... | collective-permute-start | bytes 393224 | tf_op jit(solution)/shard_map/ppermute | solution.py:22
